TPU v7x, 128 devices: a whole 4x4x4 slice. The times are simulated.
128 devices in a mesh: ctx: 16 (over y, x_lo, core), pb: 8 (over z, x_hi).
Axes of the slice: x: 4 (x_hi: 2, x_lo: 2; x = x_hi * 2 + x_lo), y: 4, z: 4, core: 2. Of those that a mesh axis runs over, the one named last changes fastest.
Arguments:
- embed_prev: bfloat16 [4096, 2048], P('ctx'), may hold values from -16 to 16
- w_query: bfloat16 [2048, 2048], P(None, 'pb'), may hold values from -1 to 1
- w_key: bfloat16 [2048, 2048], P(None, 'pb'), may hold values from -1 to 1
- w_value: bfloat16 [2048, 2048], P(None, 'pb'), may hold values from -0.125 to 0.125
- w_out: bfloat16 [2048, 2048], P('pb'), may hold values from -1 to 1
- byte_ids: int32 [4096, 8], P(('ctx', 'pb')), may hold values from 0 to 255
- pad_embed: bfloat16 [512], replicated, may hold values from -3 to 3
- byte_table: bfloat16 [256, 512], replicated, may hold values from -5 to 5
- w_link: bfloat16 [256, 512], replicated, may hold values from -0.375 to 0.375
- w_local_qkv: bfloat16 [512, 1536], replicated, may hold values from -1 to 1
- w_local_out: bfloat16 [512, 512], replicated, may hold values from -0.25 to 0.25
- w_vocab: bfloat16 [512, 256], replicated, may hold values from -3 to 3
Outputs:
- grad_query: bfloat16 [2048, 2048], P('ctx', 'pb')
- grad_key: bfloat16 [2048, 2048], P('ctx', 'pb')
- grad_value: bfloat16 [2048, 2048], P('ctx', 'pb')
- grad_out: bfloat16 [2048, 2048], P('pb', 'ctx')
All inputs are finite; a program needn't handle non-finite values.
Results may differ from a plain program's by a relative error of at most 0.035.
Values may be sent and summed in bfloat16 or wider, within the bound.
A program may use at most 128 MiB of HBM per device.

v0:
```python
import functools

import jax
import jax.numpy as jnp
from jax import lax
from jax.experimental import pallas as pl
from jax.experimental.pallas import tpu as pltpu
from jax.sharding import PartitionSpec as P

HD = 128
LHD = 64
PATCH = 8
EPSILON = 1e-06
MASKED = -1e30
MESH = pl.DeviceIdType.MESH
BF = jnp.bfloat16
F32 = jnp.float32


def nn(left, right):
    return lax.dot_general(left, right, (((1,), (0,)), ((), ())), preferred_element_type=F32)


def nt(left, right):
    return lax.dot_general(left, right, (((1,), (1,)), ((), ())), preferred_element_type=F32)


def tn(left, right):
    return lax.dot_general(left, right, (((0,), (0,)), ((), ())), preferred_element_type=F32)


def loop(low, high, body):
    def step(index, unused):
        body(index)
        return unused

    lax.fori_loop(low, high, step, 0)


def row_form(column, rows):
    return jnp.transpose(jnp.broadcast_to(column, (rows, HD)))[0:8]


def rms_inverse(values):
    return lax.rsqrt(jnp.mean(values * values, axis=1, keepdims=True) + EPSILON)


def rms_back(values, inverse, grad):
    width = values.shape[1]
    dots = jnp.sum(grad * values, axis=1, keepdims=True)
    return inverse * grad - values * (inverse * inverse * inverse * dots * (1.0 / width))


def step_kernel(
    sizes,
    embed_far,
    w_query_far,
    w_key_far,
    w_value_far,
    w_out_far,
    ids,
    pad_embed,
    table_far,
    w_link_far,
    w_mix_far,
    w_local_out_far,
    w_vocab_far,
    tall_sums,
    wide_sums,
    w_query,
    w_key,
    w_value,
    w_out,
    table,
    w_link,
    w_mix,
    w_local_out,
    w_vocab,
    load_s,
    inputs,
    row_scale,
    inputs_turned,
    kv_send,
    kv_all,
    q_send,
    q_all,
    run_max,
    run_sum,
    run_out,
    att_head,
    att_pair,
    lse_col,
    lse_all,
    glob_part,
    glob_in,
    hidden,
    mixed,
    weights,
    d_weights,
    d_mixed,
    ids_wide,
    targets_all,
    grad_all,
    da_send,
    da_all,
    dq_acc,
    dk_acc,
    dv_acc,
    wo_send,
    wq_send,
    wkv_send,
    wo_in,
    wq_in,
    wkv_in,
    kv_s,
    kv_r,
    q_s,
    q_r,
    wo_s,
    wo_r,
    wq_s,
    wq_r,
    wkv_s,
    wkv_r,
    lse_s,
    lse_r,
    glob_s,
    glob_r,
    grad_s,
    grad_r,
    norm_s,
    norm_r,
    att_s,
    att_r,
    full_s,
    full_r,
    da_s,
    da_r,
    kv_forward_s,
    da_forward_s,
):
    nctx, npb = sizes
    chips = nctx // 2
    rows, wide = embed_far.shape
    patches = rows // npb
    bytes_here = patches * PATCH
    scale = HD ** (-0.5)
    place = lax.axis_index("ctx")
    part = lax.axis_index("pb")
    chip = lax.div(place, 2)
    core = lax.rem(place, 2)
    other = place + 1 - 2 * core

    def ctx_copy(src, dst, send, recv, peer):
        return pltpu.make_async_remote_copy(
            src_ref=src,
            dst_ref=dst,
            send_sem=send,
            recv_sem=recv,
            device_id=(peer, part),
            device_id_type=MESH,
        )

    def pb_copy(src, dst, send, recv, peer):
        return pltpu.make_async_remote_copy(
            src_ref=src,
            dst_ref=dst,
            send_sem=send,
            recv_sem=recv,
            device_id=(place, peer),
            device_id_type=MESH,
        )

    def each_peer(wanted, action):
        def one(step):
            peer = lax.rem(place + nctx - step, nctx)

            @pl.when(wanted(lax.div(peer, 2)))
            def _():
                action(peer)

        loop(1, nctx, one)

    def each_part(action):
        loop(1, npb, lambda step: action(lax.rem(part + step, npb)))

    half_rows = rows // 2
    pairs_in = (
        (embed_far.at[0:half_rows], inputs.at[core, 0:half_rows]),
        (embed_far.at[half_rows:rows], inputs.at[core, half_rows:rows]),
        (w_key_far, w_key),
        (w_value_far, w_value),
        (w_query_far, w_query),
        (w_out_far, w_out),
        (table_far, table),
        (w_link_far, w_link),
        (w_mix_far, w_mix),
        (w_local_out_far, w_local_out),
        (w_vocab_far, w_vocab),
    )
    loads = [
        pltpu.make_async_copy(far, near, load_s.at[index])
        for index, (far, near) in enumerate(pairs_in)
    ]
    for load in loads[:4]:
        load.start()

    later = lambda at: at >= chip
    earlier = lambda at: at <= chip
    anyone = lambda at: at >= 0

    def crossing(at, rows_away):
        return jnp.logical_and(lax.div(at, 2) - lax.div(chip, 2) == rows_away, lax.rem(at, 2) != lax.rem(chip, 2))

    later_direct = lambda at: jnp.logical_and(later(at), jnp.logical_not(crossing(at, 2)))
    earlier_direct = lambda at: jnp.logical_and(earlier(at), jnp.logical_not(crossing(at, -2)))
    neighbour = 2 * (chip + 1 - 2 * lax.rem(chip, 2)) + core

    barrier = pltpu.get_barrier_semaphore()

    def greet_ctx(peer):
        pl.semaphore_signal(barrier, inc=1, device_id=(peer, part), device_id_type=MESH)

    def greet_part(peer):
        pl.semaphore_signal(barrier, inc=1, device_id=(place, peer), device_id_type=MESH)

    each_peer(anyone, greet_ctx)
    each_part(greet_part)

    tile_rows = min(32, rows)

    def scale_rows(index):
        for low in range(0, rows, tile_rows):
            values = inputs[index, low : low + tile_rows, :].astype(F32)
            row_scale[index, low : low + tile_rows] = jnp.broadcast_to(
                rms_inverse(values), (tile_rows, HD)
            )

    loads[0].wait()
    loads[1].wait()
    loads[4].start()
    scale_rows(core)
    own_inputs = inputs[core]

    def scaled(product):
        return (product * row_scale[core, :, 0:1]).astype(BF)

    for slot, weight in ((0, w_key), (1, w_value)):
        loads[2 + slot].wait()
        product = scaled(nn(own_inputs, weight[...]))
        kv_send[0, slot] = product[:, :HD]
        kv_send[1, slot] = product[:, HD:]
    pl.semaphore_wait(barrier, nctx + npb - 2)

    def kv_copy(peer):
        return ctx_copy(
            kv_send.at[lax.rem(peer, 2)], kv_all.at[:, place], kv_s.at[peer], kv_r.at[place], peer
        )

    def kv_start(step):
        peer = lax.rem(place + step, nctx)

        @pl.when(later_direct(lax.div(peer, 2)))
        def _():
            kv_copy(peer).start()

    loop(1, nctx, kv_start)
    for load in loads[5:]:
        load.start()
    kv_all[:, place] = kv_send[core]
    loads[4].wait()
    product = scaled(nn(own_inputs, w_query[...]))
    q_send[0] = product[:, :HD]
    q_send[1] = product[:, HD:]

    def q_copy(peer):
        return ctx_copy(q_send.at[lax.rem(peer, 2)], q_all.at[place], q_s.at[peer], q_r.at[place], peer)

    q_copy(other).start()
    q_all[place] = q_send[core]

    def norm_copy(index):
        return ctx_copy(inputs.at[index], inputs.at[index], norm_s, norm_r, other)

    norm_copy(core).start()
    strictly_earlier = lambda at: at < chip
    each_peer(strictly_earlier, lambda peer: q_copy(peer).start())

    def kv_wait(peer):
        ctx_copy(kv_send.at[0], kv_all.at[:, peer], kv_s.at[peer], kv_r.at[peer], peer).wait_recv()

    def q_wait(peer):
        ctx_copy(q_send.at[0], q_all.at[peer], q_s.at[peer], q_r.at[peer], peer).wait_recv()

    first = 2 * chip
    pair_rows = 2 * rows

    def keys_of(at):
        return kv_all[0, pl.ds(2 * at, 2)].reshape(pair_rows, HD)

    def values_of(at):
        return kv_all[1, pl.ds(2 * at, 2)].reshape(pair_rows, HD)

    def diagonal(half, keys_down):
        shape = (rows, pair_rows)
        here = lax.broadcasted_iota(jnp.int32, shape, 0) + half * rows
        there = lax.broadcasted_iota(jnp.int32, shape, 1)
        return (there >= here) if keys_down else (there <= here)

    run_max[...] = jnp.full(run_max.shape, MASKED, F32)
    run_sum[...] = jnp.zeros(run_sum.shape, F32)
    run_out[...] = jnp.zeros(run_out.shape, F32)

    def attend(half, at, on_diagonal):
        scores = nt(q_all[first + half], keys_of(at)) * scale
        if on_diagonal:
            scores = jnp.where(diagonal(half, False), scores, MASKED)
        before = run_max[half, :, 0:1]
        highest = jnp.maximum(before, jnp.max(scores, axis=1, keepdims=True))
        exps = jnp.exp(scores - highest)
        factor = jnp.exp(before - highest)
        total = run_sum[half, :, 0:1] * factor + jnp.sum(exps, axis=1, keepdims=True)
        run_out[half] = run_out[half] * factor + nn(exps.astype(BF), values_of(at))
        run_max[half] = jnp.broadcast_to(highest, (rows, HD))
        run_sum[half] = jnp.broadcast_to(total, (rows, HD))

    kv_wait(other)
    q_wait(other)
    for half in (0, 1):
        attend(half, chip, True)
    norm_copy(1 - core).wait_recv()
    scale_rows(1 - core)
    turn_tile = min(128, wide)

    def turn_columns(step):
        here = pl.ds(pl.multiple_of(step * turn_tile, turn_tile), turn_tile)
        block = inputs[:, :, here].reshape(pair_rows, turn_tile)
        inputs_turned[here, :] = jnp.transpose(block.astype(F32)).astype(BF)

    loop(0, wide // turn_tile, turn_columns)
    for load in loads[5:]:
        load.wait()

    def kv_forward(side):
        source = 2 * (chip - 4) + side
        block = kv_all.at[:, source]
        return ctx_copy(block, block, kv_forward_s.at[side], kv_r.at[source], neighbour)

    @pl.when(chip >= 4)
    def _():
        for side in (0, 1):
            kv_wait(2 * (chip - 4) + side)
            kv_forward(side).start()
        for half in (0, 1):
            attend(half, chip - 4, False)

    def attend_earlier(step):
        at = chip - step

        @pl.when(step != 4)
        def _():
            kv_wait(2 * at)
            kv_wait(2 * at + 1)
            for half in (0, 1):
                attend(half, at, False)

    loop(1, chip + 1, attend_earlier)
    for half in (0, 1):
        att_head[half] = (run_out[half] / run_sum[half]).astype(BF)
        log_total = run_max[half] + jnp.log(run_sum[half])
        lse_col[half] = log_total
        lse_all[chip, half] = jnp.transpose(log_total)[0:8]

    def att_copy():
        return ctx_copy(att_head.at[1 - core], att_pair.at[core], att_s, att_r, other)

    att_copy().start()
    att_pair[core] = att_head[core]

    def lse_copy(at):
        return ctx_copy(
            lse_all.at[chip], lse_all.at[chip], lse_s.at[at], lse_r.at[chip], 2 * at + core
        )

    loop(0, chip, lambda at: lse_copy(at).start())
    ctx_copy(att_head.at[0], att_pair.at[1 - core], att_s, att_r, other).wait_recv()

    both_heads = jnp.concatenate([att_pair[0], att_pair[1]], axis=1)
    out_tile = min(512, wide)

    def out_columns(step):
        here = pl.ds(pl.multiple_of(step * out_tile, out_tile), out_tile)
        product = nn(both_heads, w_out[:, here]).astype(BF)
        glob_part[:, :, here] = product.reshape(npb, patches, out_tile)

    loop(0, wide // out_tile, out_columns)

    groups = 2
    share = patches // groups

    def glob_copy(group, peer):
        here = pl.ds(pl.multiple_of(group * share, share), share)
        return pb_copy(
            glob_part.at[peer, here],
            glob_in.at[part, here],
            glob_s.at[group, peer],
            glob_r.at[group, part],
            peer,
        )

    def glob_wait(group, peer):
        here = pl.ds(pl.multiple_of(group * share, share), share)
        pb_copy(
            glob_part.at[0, here],
            glob_in.at[peer, here],
            glob_s.at[group, peer],
            glob_r.at[group, peer],
            peer,
        ).wait_recv()

    for group in range(groups):
        each_part(lambda peer: glob_copy(group, peer).start())
    glob_in[part] = glob_part[part]

    count = share * PATCH
    byte_wide = wide // PATCH
    local_wide = w_link.shape[1]
    pairs = local_wide // (2 * LHD)
    symbols = lax.broadcasted_iota(jnp.int32, (count, table.shape[0]), 1)
    nothing = jnp.full((share, 1), -1, jnp.int32)
    ids_wide[:, 0:patches] = ids[...]
    for group in range(groups):
        columns = []
        for b in range(PATCH):
            line = jnp.broadcast_to(ids_wide[b : b + 1, :], (HD, HD))
            columns.append(jnp.transpose(line)[group * share : (group + 1) * share, 0:1])
        preceding = jnp.concatenate([nothing] + columns[:-1], axis=0)
        targets_all[group] = jnp.broadcast_to(jnp.concatenate(columns, axis=0), (count, HD))
        hidden[group] = nn((preceding == symbols).astype(BF), table[...]) + jnp.where(
            preceding < 0, pad_embed[...].astype(F32).reshape(1, local_wide), 0.0
        )
    row_index = lax.broadcasted_iota(jnp.int32, (count, count), 0)
    column_index = lax.broadcasted_iota(jnp.int32, (count, count), 1)
    same = jnp.logical_and(
        lax.rem(row_index, share) == lax.rem(column_index, share), column_index <= row_index
    )
    lane = lax.broadcasted_iota(jnp.int32, (count, 2 * LHD), 1)
    halves = (lane < LHD, lane >= LHD)

    def pair_of(block, pair):
        low = block * local_wide + pair * 2 * LHD
        return mixed[:, low : low + 2 * LHD]

    def kept(values, side):
        return jnp.where(halves[side], values, jnp.zeros_like(values))

    def grad_copy(group, peer):
        mine = grad_all.at[core, part, pl.ds(pl.multiple_of(group * share, share), share)]
        return pb_copy(mine, mine, grad_s.at[group, peer], grad_r.at[group, part], peer)

    def grad_wait(group, peer):
        theirs = grad_all.at[core, peer, pl.ds(pl.multiple_of(group * share, share), share)]
        pb_copy(theirs, theirs, grad_s.at[group, peer], grad_r.at[group, peer], peer).wait_recv()

    def local_model(group):
        here = pl.ds(pl.multiple_of(group * share, share), share)
        each_part(lambda peer: glob_wait(group, peer))
        glob = glob_in[0, here, :].astype(F32)
        for index in range(1, npb):
            glob = glob + glob_in[index, here, :].astype(F32)
        glob = glob.astype(BF)
        pieces = jnp.concatenate(
            [glob[:, b * byte_wide : (b + 1) * byte_wide] for b in range(PATCH)], axis=0
        )
        hidden_one = hidden[group] + nn(pieces, w_link[...])
        hidden[group] = hidden_one
        inverse_one = rms_inverse(hidden_one)
        mixed[...] = nn((hidden_one * inverse_one).astype(BF), w_mix[...]).astype(BF)
        heads = 2 * pairs
        for head in range(heads):
            query = kept(pair_of(0, head // 2), head % 2)
            weights[head] = nt(query, pair_of(1, head // 2))
        scores = jnp.where(same[None], weights[...] * LHD ** (-0.5), MASKED)
        exps = jnp.exp(scores - jnp.max(scores, axis=2, keepdims=True))
        weights[...] = exps / jnp.sum(exps, axis=2, keepdims=True)
        local_att = []
        for pair in range(pairs):
            terms = [
                nn(weights[2 * pair + side].astype(BF), kept(pair_of(2, pair), side))
                for side in (0, 1)
            ]
            local_att.append((terms[0] + terms[1]).astype(BF))
        hidden_two = hidden[group] + nn(jnp.concatenate(local_att, axis=1), w_local_out[...])
        inverse_two = rms_inverse(hidden_two)
        logits = nn((hidden_two * inverse_two).astype(BF), w_vocab[...])
        exps = jnp.exp(logits - jnp.max(logits, axis=1, keepdims=True))
        soft = exps / jnp.sum(exps, axis=1, keepdims=True)
        d_logits = (
            soft - jnp.where(targets_all[group, :, 0:1] == symbols, 1.0, 0.0)
        ) * (1.0 / (rows * nctx * PATCH))
        d_normed_two = nt(d_logits.astype(BF), w_vocab[...]).astype(BF).astype(F32)
        d_hidden = rms_back(hidden_two, inverse_two, d_normed_two)
        d_local_att = nt(d_hidden.astype(BF), w_local_out[...]).astype(BF)
        d_heads = [
            kept(d_local_att[:, pair * 2 * LHD : (pair + 1) * 2 * LHD], side)
            for pair in range(pairs)
            for side in (0, 1)
        ]
        for head in range(heads):
            d_weights[head] = nt(d_heads[head], pair_of(2, head // 2))
        d_soft = d_weights[...].astype(BF).astype(F32)
        soft = weights[...]
        dots = jnp.sum(d_soft * soft, axis=2, keepdims=True)
        d_weights[...] = soft * (d_soft - dots) * LHD ** (-0.5)
        for pair in range(pairs):
            terms = [[], [], []]
            for side in (0, 1):
                head = 2 * pair + side
                d_scores = d_weights[head].astype(BF)
                terms[0].append(nn(d_scores, kept(pair_of(1, pair), side)))
                terms[1].append(tn(d_scores, kept(pair_of(0, pair), side)))
                terms[2].append(tn(weights[head].astype(BF), d_heads[head]))
            for block in range(3):
                at = block * local_wide + pair * 2 * LHD
                d_mixed[:, at : at + 2 * LHD] = (terms[block][0] + terms[block][1]).astype(BF)
        d_normed_one = nt(d_mixed[...], w_mix[...]).astype(BF).astype(F32)
        hidden_one = hidden[group]
        d_hidden = d_hidden + rms_back(hidden_one, rms_inverse(hidden_one), d_normed_one)
        d_pieces = nt(d_hidden.astype(BF), w_link[...]).astype(BF)
        for b in range(PATCH):
            grad_all[core, part, here, b * byte_wide : (b + 1) * byte_wide] = d_pieces[
                b * share : (b + 1) * share
            ]
        each_part(lambda peer: grad_copy(group, peer).start())

    each_peer(later_direct, lambda peer: kv_copy(peer).wait_send())

    @pl.when(chip >= 4)
    def _():
        for side in (0, 1):
            kv_forward(side).wait_send()

    each_peer(earlier, lambda peer: q_copy(peer).wait_send())
    loop(0, chip, lambda at: lse_copy(at).wait_send())
    norm_copy(core).wait_send()
    att_copy().wait_send()

    loop(0, groups, local_model)
    def full_copy(group, index):
        here = pl.ds(group * share, share)
        block = grad_all.at[index, :, here]
        return ctx_copy(block, block, full_s.at[group], full_r.at[group], other)

    last = groups - 1

    def da_parts(group, whole):
        return whole.at[0 : npb + 1 if group == last else npb, group * share : (group + 1) * share]

    def da_copy(group, peer):
        return ctx_copy(
            da_parts(group, da_send.at[lax.rem(peer, 2)]),
            da_parts(group, da_all.at[place]),
            da_s.at[group, peer],
            da_r.at[group, place],
            peer,
        )

    def da_wait_part(group, peer):
        ctx_copy(
            da_parts(group, da_send.at[0]),
            da_parts(group, da_all.at[peer]),
            da_s.at[group, peer],
            da_r.at[group, peer],
            peer,
        ).wait_recv()

    def da_wait(peer):
        for group in range(groups):
            da_wait_part(group, peer)

    def da_forward(group, side):
        source = 2 * (chip + 4) + side
        block = da_parts(group, da_all.at[source])
        return ctx_copy(
            block, block, da_forward_s.at[group, side], da_r.at[group, source], neighbour
        )

    for group in range(groups):
        each_part(lambda peer: grad_wait(group, peer))
        full_copy(group, core).start()
        here = slice(group * share, (group + 1) * share)
        grads = grad_all[core, :, here, :].reshape(npb * share, wide)
        product = nt(grads, w_out[...]).astype(BF)
        for head in (0, 1):
            d_att = product[:, head * HD : (head + 1) * HD]
            da_send[head, 0:npb, here, :] = d_att.reshape(npb, share, HD)
        if group == last:
            for head in (0, 1):
                d_att = da_send[head, 0:npb].reshape(rows, HD).astype(F32)
                dots = jnp.sum(d_att * att_pair[head].astype(F32), axis=1, keepdims=True)
                exact = row_form(dots, rows)
                high = exact.astype(BF)
                low = (exact - high.astype(F32)).astype(BF)
                spare = jnp.concatenate([high[0:1], low[0:1]], axis=0)
                tail = [spare[:, at : at + HD] for at in range(0, rows, HD)]
                filler = jnp.zeros((share - 2 * len(tail), HD), BF)
                da_send[head, npb, here, :] = jnp.concatenate(tail + [filler], axis=0)
        da_copy(group, other).start()

        def da_start(peer):
            @pl.when(earlier_direct(lax.div(peer, 2)))
            def _():
                da_copy(group, peer).start()

        loop(0, 2 * chip, da_start)

    def grads_of(device):
        return da_all[device, 0:npb].reshape(rows, HD)

    def dots_of(device):
        tail = da_all[device, npb, last * share : (last + 1) * share].astype(F32)
        pieces = [
            tail[2 * at : 2 * at + 1] + tail[2 * at + 1 : 2 * at + 2] for at in range(rows // HD)
        ]
        return jnp.concatenate(pieces, axis=1)

    da_all[place] = da_send[core]

    block_wide = wide // nctx
    term_rows = min(512, wide)
    owners = term_rows // block_wide

    def wo_copy(peer):
        return ctx_copy(wo_send.at[peer], wo_in.at[place], wo_s.at[peer], wo_r.at[place], peer)

    def wq_copy(peer):
        return ctx_copy(wq_send.at[peer], wq_in.at[place], wq_s.at[peer], wq_r.at[place], peer)

    def wkv_copy(peer):
        return ctx_copy(wkv_send.at[peer], wkv_in.at[place], wkv_s.at[peer], wkv_r.at[place], peer)

    def in_turn(make, copy):
        steps = wide // term_rows

        def one(step):
            block = lax.rem(lax.div(place, owners) + step, steps)
            make(block)
            for index in range(owners):
                peer = block * owners + index

                @pl.when(peer != place)
                def _():
                    copy(peer).start()

        loop(0, steps, one)

    for group in range(groups):
        full_copy(group, 1 - core).wait_recv()
    att_turned = jnp.transpose(att_head[...].reshape(pair_rows, HD).astype(F32)).astype(BF)

    def wo_block(step):
        here = pl.ds(pl.multiple_of(step * term_rows, term_rows), term_rows)
        grads = grad_all[:, :, :, here].reshape(pair_rows, term_rows)
        terms = nn(att_turned, grads).astype(BF)
        for index in range(owners):
            wo_send[step * owners + index] = terms[:, index * block_wide : (index + 1) * block_wide]

    in_turn(wo_block, wo_copy)
    wo_in[place] = wo_send[place]
    da_wait(other)

    dq_acc[...] = jnp.zeros(dq_acc.shape, F32)

    def query_back(half, at, on_diagonal):
        scores = nt(q_all[first + half], keys_of(at)) * scale
        probs = jnp.exp(scores - lse_col[half, :, 0:1])
        if on_diagonal:
            probs = jnp.where(diagonal(half, False), probs, 0.0)
        d_probs = nt(grads_of(first + half), values_of(at))
        d_scores = (probs * (d_probs - run_sum[half, :, 0:1]) * scale).astype(BF)
        dq_acc[half] += nn(d_scores, keys_of(at))

    for half in (0, 1):
        dots = jnp.sum(
            grads_of(first + half).astype(F32) * att_head[half].astype(F32), axis=1, keepdims=True
        )
        run_sum[half] = jnp.broadcast_to(dots, (rows, HD))
    for half in (0, 1):
        query_back(half, chip, True)

    def query_earlier(step):
        for half in (0, 1):
            query_back(half, chip - step, False)

    loop(1, chip + 1, query_earlier)

    dq_ready = (dq_acc[...] * row_scale[...]).reshape(pair_rows, HD).astype(BF)

    def wq_block(step):
        here = pl.ds(pl.multiple_of(step * term_rows, term_rows), term_rows)
        terms = nn(inputs_turned[here, :], dq_ready).astype(BF)
        wq_send[pl.ds(step * owners, owners)] = terms.reshape(owners, block_wide, HD)

    in_turn(wq_block, wq_copy)
    wq_in[place] = wq_send[place]

    dk_acc[...] = jnp.zeros(dk_acc.shape, F32)
    dv_acc[...] = jnp.zeros(dv_acc.shape, F32)

    def key_back(half, at, on_diagonal):
        queries = q_all[pl.ds(2 * at, 2)].reshape(pair_rows, HD)
        grads = da_all[pl.ds(2 * at, 2), 0:npb].reshape(pair_rows, HD)
        log_total = jnp.concatenate([lse_all[at, 0, 0:1, :], lse_all[at, 1, 0:1, :]], axis=1)
        dots = jnp.concatenate([dots_of(2 * at), dots_of(2 * at + 1)], axis=1)
        scores = nt(kv_all[0, first + half], queries) * scale
        probs = jnp.exp(scores - log_total)
        if on_diagonal:
            probs = jnp.where(diagonal(half, True), probs, 0.0)
        d_probs = nt(kv_all[1, first + half], grads)
        d_scores = (probs * (d_probs - dots) * scale).astype(BF)
        dv_acc[half] += nn(probs.astype(BF), grads)
        dk_acc[half] += nn(d_scores, queries)

    for half in (0, 1):
        key_back(half, chip, True)

    def rest_wait(at):
        q_wait(2 * at)
        q_wait(2 * at + 1)
        ctx_copy(
            lse_all.at[at], lse_all.at[at], lse_s.at[at], lse_r.at[at], 2 * at + core
        ).wait_recv()

    @pl.when(chip < chips - 4)
    def _():
        for group in range(groups):
            for side in (0, 1):
                da_wait_part(group, 2 * (chip + 4) + side)
                da_forward(group, side).start()
        rest_wait(chip + 4)
        for half in (0, 1):
            key_back(half, chip + 4, False)

    def key_later(at):
        @pl.when(at != chip + 4)
        def _():
            da_wait(2 * at)
            da_wait(2 * at + 1)
            rest_wait(at)
            for half in (0, 1):
                key_back(half, at, False)

    loop(chip + 1, chips, key_later)
    dkv_ready = jnp.concatenate(
        [
            (total[...] * row_scale[...]).reshape(pair_rows, HD).astype(BF)
            for total in (dk_acc, dv_acc)
        ],
        axis=1,
    )

    def wkv_block(step):
        here = pl.ds(pl.multiple_of(step * term_rows, term_rows), term_rows)
        terms = nn(inputs_turned[here, :], dkv_ready).astype(BF)
        wkv_send[pl.ds(step * owners, owners)] = terms.reshape(owners, block_wide, 2 * HD)

    in_turn(wkv_block, wkv_copy)
    wkv_in[place] = wkv_send[place]

    def sent_part(peer):
        for group in range(groups):
            glob_copy(group, peer).wait_send()
            grad_copy(group, peer).wait_send()

    each_part(sent_part)

    def sent_earlier(peer):
        for group in range(groups):
            da_copy(group, peer).wait_send()

    each_peer(earlier_direct, sent_earlier)

    @pl.when(chip < chips - 4)
    def _():
        for side in (0, 1):
            for group in range(groups):
                da_forward(group, side).wait_send()

    for group in range(groups):
        full_copy(group, core).wait_send()

    def sent_all(peer):
        wo_copy(peer).wait_send()
        wq_copy(peer).wait_send()
        wkv_copy(peer).wait_send()

    def total_of(pick, head):
        total = pick(head).astype(F32)
        for index in range(1, chips):
            total = total + pick(2 * index + head).astype(F32)
        return total.astype(BF)

    def wo_wait(peer):
        ctx_copy(wo_send.at[0], wo_in.at[peer], wo_s.at[peer], wo_r.at[peer], peer).wait_recv()

    def wq_wait(peer):
        ctx_copy(wq_send.at[0], wq_in.at[peer], wq_s.at[peer], wq_r.at[peer], peer).wait_recv()

    def wkv_wait(peer):
        ctx_copy(wkv_send.at[0], wkv_in.at[peer], wkv_s.at[peer], wkv_r.at[peer], peer).wait_recv()

    each_peer(anyone, wo_wait)
    for head in (0, 1):
        wide_sums[head * HD : (head + 1) * HD, :] = total_of(lambda index: wo_in[index], head)
    each_peer(anyone, wq_wait)
    for head in (0, 1):
        at = head * HD
        tall_sums[0, :, at : at + HD] = total_of(lambda index: wq_in[index], head)
    each_peer(anyone, sent_all)
    each_peer(anyone, wkv_wait)
    for head in (0, 1):
        at = head * HD
        total = total_of(lambda index: wkv_in[index], head)
        tall_sums[1, :, at : at + HD] = total[:, :HD]
        tall_sums[2, :, at : at + HD] = total[:, HD:]


def split_kernel(tall_sums, wide_sums, grad_query, grad_key, grad_value, grad_out):
    grad_query[...] = tall_sums[0]
    grad_key[...] = tall_sums[1]
    grad_value[...] = tall_sums[2]
    grad_out[...] = wide_sums[...]


def per_device(nctx, npb, *args):
    embed, w_query, w_key, w_value, w_out, ids, pad_embed, table, w_link, w_mix, w_lo, w_vocab = args
    rows, wide = embed.shape
    patches = rows // npb
    groups = 2
    local_rows = patches // groups * PATCH
    local_wide = w_link.shape[1]
    chips = nctx // 2
    block = wide // nctx
    vmem = pltpu.VMEM
    dma = pltpu.SemaphoreType.DMA
    near = [w_query, w_key, w_value, w_out, table, w_link, w_mix, w_lo, w_vocab]
    scratch = [vmem(array.shape, BF) for array in near]
    scratch += [
        dma((len(near) + 2,)),
        vmem((2, rows, wide), BF),
        vmem((2, rows, HD), F32),
        vmem((wide, 2 * rows), BF),
        vmem((2, 2, rows, HD), BF),
        vmem((2, nctx, rows, HD), BF),
        vmem((2, rows, HD), BF),
        vmem((nctx, rows, HD), BF),
        vmem((2, rows, HD), F32),
        vmem((2, rows, HD), F32),
        vmem((2, rows, HD), F32),
        vmem((2, rows, HD), BF),
        vmem((2, rows, HD), BF),
        vmem((2, rows, HD), F32),
        vmem((chips, 2, 8, rows), F32),
        vmem((npb, patches, wide), BF),
        vmem((npb, patches, wide), BF),
        vmem((groups, local_rows, local_wide), F32),
        vmem((local_rows, 3 * local_wide), BF),
        vmem((local_wide // LHD, local_rows, local_rows), F32),
        vmem((local_wide // LHD, local_rows, local_rows), F32),
        vmem((local_rows, 3 * local_wide), BF),
        vmem((PATCH, HD), jnp.int32),
        vmem((groups, local_rows, HD), jnp.int32),
        vmem((2, npb, patches, wide), BF),
        vmem((2, npb + 1, patches, HD), BF),
        vmem((nctx, npb + 1, patches, HD), BF),
        vmem((2, rows, HD), F32),
        vmem((2, rows, HD), F32),
        vmem((2, rows, HD), F32),
        vmem((nctx, HD, block), BF),
        vmem((nctx, block, HD), BF),
        vmem((nctx, block, 2 * HD), BF),
        vmem((nctx, HD, block), BF),
        vmem((nctx, block, HD), BF),
        vmem((nctx, block, 2 * HD), BF),
    ]
    scratch += [dma((nctx,))] * 10
    scratch += [dma((chips,))] * 2
    scratch += [dma((groups, npb))] * 4
    scratch += [dma] * 4 + [dma((groups,))] * 2 + [dma((groups, nctx))] * 2
    scratch += [dma((2,)), dma((groups, 2))]
    whole = pl.BlockSpec(memory_space=pltpu.VMEM)
    far = pl.BlockSpec(memory_space=pl.ANY)
    tall = jax.ShapeDtypeStruct((block, 2 * HD), BF)
    sums = pl.pallas_call(
        functools.partial(step_kernel, (nctx, npb)),
        out_shape=(
            jax.ShapeDtypeStruct((3, block, 2 * HD), BF),
            jax.ShapeDtypeStruct((2 * HD, block), BF),
        ),
        in_specs=[far] * 5 + [whole] * 2 + [far] * 5,
        out_specs=(whole,) * 2,
        scratch_shapes=scratch,
        compiler_params=pltpu.CompilerParams(
            collective_id=0, has_side_effects=True, vmem_limit_bytes=56 * 1024 * 1024
        ),
        name="step",
    )(
        embed, w_query, w_key, w_value, w_out, ids.T, pad_embed, table, w_link, w_mix,
        w_lo, w_vocab,
    )
    return pl.pallas_call(
        split_kernel,
        out_shape=(tall, tall, tall, jax.ShapeDtypeStruct((2 * HD, block), BF)),
        in_specs=[whole] * 2,
        out_specs=(whole,) * 4,
        name="split",
    )(*sums)


def solution(mesh):
    in_specs = (
        P("ctx", None),
        P(None, "pb"),
        P(None, "pb"),
        P(None, "pb"),
        P("pb", None),
        P(("ctx", "pb"), None),
        P(),
        P(),
        P(),
        P(),
        P(),
        P(),
    )
    out_specs = (P("ctx", "pb"), P("ctx", "pb"), P("ctx", "pb"), P("pb", "ctx"))
    return jax.shard_map(
        functools.partial(per_device, mesh.shape["ctx"], mesh.shape["pb"]),
        mesh=mesh,
        in_specs=in_specs,
        out_specs=out_specs,
        check_vma=False,
    )
```

profile of v0, /device:TPU:9, one launch (start us, length us, event | category | flops | bytes accessed | tf_op | source)
XLA Modules:
  0.0 98.0 jit_solution(15683973293581611922)
XLA Ops:
  0.6 95.7 %step.1 = (bf16[3,128,256]{2,1,0:T(8,128)(2,1)}, bf16[256,128]{1,0:T(8,128)(2,1)}) custom-call(bf16[256,2048]{1,0:T(8,128)(2,1)} %embed_far.1, bf16[2048,256]{1,0:T(8,128)(2,1)} %w_query_far.1, bf16[2048,256]{1,0:T(8,128)(2,1)} %w_key_far.1, bf16[2048,256]{1,0:T(8,128)(2,1)} %w_value_far.1, bf16[256,2048]{1,0:T(8,128)(2,1)} %w_out_far.1, s32[8,32]{1,0:T(8,128)} %bitcast.1, ...), custom_call_target="tpu_custom_call" | custom-call | tf_op jit(solution)/shard_map/step/pallas_call | solution.py:894
  96.4 1.6 %split.1 = (bf16[128,256]{1,0:T(8,128)(2,1)}, bf16[128,256]{1,0:T(8,128)(2,1)}, bf16[128,256]{1,0:T(8,128)(2,1)}, bf16[256,128]{1,0:T(8,128)(2,1)}) custom-call(bf16[3,128,256]{2,1,0:T(8,128)(2,1)} %get-tuple-element.6.tall_sums, bf16[256,128]{1,0:T(8,128)(2,1)} %get-tuple-element.7.wide_sums), custom_call_target="tpu_custom_call" | custom-call | tf_op jit(solution)/shard_map/split/pallas_call | solution.py:911
where the time goes:
time: 98.6 us; the launch traced here: 98 us
  Pallas kernels  97.4 us (99%)
    pallas_call x1, Pallas kernels, per_device(): pl.pallas_call(functools.partial(step_kernel, (nctx, npb)), out_shape=(ja...  95.7 us

commit v1 on v0

--- a/solution.py
+++ b/solution.py
@@ -259,10 +259,16 @@
 
     def kv_start(step):
         peer = lax.rem(place + step, nctx)
-
-        @pl.when(later_direct(lax.div(peer, 2)))
+        at = lax.div(peer, 2)
+
+        @pl.when(jnp.logical_and(later_direct(at), at != chip + 4))
         def _():
             kv_copy(peer).start()
+
+    @pl.when(chip < chips - 4)
+    def _():
+        for side in (0, 1):
+            kv_copy(2 * (chip + 4) + side).start()
 
     loop(1, nctx, kv_start)
     for load in loads[5:]:

time: 98.6 us -> 98 us (level)
  no operation moved by 1% of the time
where the time goes in v1:
time: 98 us; the launch traced here: 97.8 us
  Pallas kernels  97.2 us (99%)
    pallas_call x1, Pallas kernels, per_device(): pl.pallas_call(functools.partial(step_kernel, (nctx, npb)), out_shape=(ja...  95.5 us

profile of v1, /device:TPU:9, one launch (start us, length us, event | category | flops | bytes accessed | tf_op | source)
XLA Modules:
  0.0 97.8 jit_solution(14386951257330860927)
XLA Ops:
  0.6 95.5 %step.1 = (bf16[3,128,256]{2,1,0:T(8,128)(2,1)}, bf16[256,128]{1,0:T(8,128)(2,1)}) custom-call(bf16[256,2048]{1,0:T(8,128)(2,1)} %embed_far.1, bf16[2048,256]{1,0:T(8,128)(2,1)} %w_query_far.1, bf16[2048,256]{1,0:T(8,128)(2,1)} %w_key_far.1, bf16[2048,256]{1,0:T(8,128)(2,1)} %w_value_far.1, bf16[256,2048]{1,0:T(8,128)(2,1)} %w_out_far.1, s32[8,32]{1,0:T(8,128)} %bitcast.1, ...), custom_call_target="tpu_custom_call" | custom-call | tf_op jit(solution)/shard_map/step/pallas_call | solution.py:900
  96.2 1.6 %split.1 = (bf16[128,256]{1,0:T(8,128)(2,1)}, bf16[128,256]{1,0:T(8,128)(2,1)}, bf16[128,256]{1,0:T(8,128)(2,1)}, bf16[256,128]{1,0:T(8,128)(2,1)}) custom-call(bf16[3,128,256]{2,1,0:T(8,128)(2,1)} %get-tuple-element.6.tall_sums, bf16[256,128]{1,0:T(8,128)(2,1)} %get-tuple-element.7.wide_sums), custom_call_target="tpu_custom_call" | custom-call | tf_op jit(solution)/shard_map/split/pallas_call | solution.py:917

commit v2 on v1

--- a/solution.py
+++ b/solution.py
@@ -334,16 +334,6 @@
     q_wait(other)
     for half in (0, 1):
         attend(half, chip, True)
-    norm_copy(1 - core).wait_recv()
-    scale_rows(1 - core)
-    turn_tile = min(128, wide)
-
-    def turn_columns(step):
-        here = pl.ds(pl.multiple_of(step * turn_tile, turn_tile), turn_tile)
-        block = inputs[:, :, here].reshape(pair_rows, turn_tile)
-        inputs_turned[here, :] = jnp.transpose(block.astype(F32)).astype(BF)
-
-    loop(0, wide // turn_tile, turn_columns)
     for load in loads[5:]:
         load.wait()
 
@@ -538,6 +528,17 @@
                 b * share : (b + 1) * share
             ]
         each_part(lambda peer: grad_copy(group, peer).start())
+
+    norm_copy(1 - core).wait_recv()
+    scale_rows(1 - core)
+    turn_tile = min(128, wide)
+
+    def turn_columns(step):
+        here = pl.ds(pl.multiple_of(step * turn_tile, turn_tile), turn_tile)
+        block = inputs[:, :, here].reshape(pair_rows, turn_tile)
+        inputs_turned[here, :] = jnp.transpose(block.astype(F32)).astype(BF)
+
+    loop(0, wide // turn_tile, turn_columns)
 
     each_peer(later_direct, lambda peer: kv_copy(peer).wait_send())
 

time: 98 us -> 98 us (level)
  no operation moved by 1% of the time
where the time goes in v2:
time: 98 us; the launch traced here: 97.8 us
  Pallas kernels  97.1 us (99%)
    pallas_call x1, Pallas kernels, per_device(): pl.pallas_call(functools.partial(step_kernel, (nctx, npb)), out_shape=(ja...  95.5 us

profile of v2, /device:TPU:9, one launch (start us, length us, event | category | flops | bytes accessed | tf_op | source)
XLA Modules:
  0.0 97.8 jit_solution(1983509161762692553)
XLA Ops:
  0.6 95.5 %step.1 = (bf16[3,128,256]{2,1,0:T(8,128)(2,1)}, bf16[256,128]{1,0:T(8,128)(2,1)}) custom-call(bf16[256,2048]{1,0:T(8,128)(2,1)} %embed_far.1, bf16[2048,256]{1,0:T(8,128)(2,1)} %w_query_far.1, bf16[2048,256]{1,0:T(8,128)(2,1)} %w_key_far.1, bf16[2048,256]{1,0:T(8,128)(2,1)} %w_value_far.1, bf16[256,2048]{1,0:T(8,128)(2,1)} %w_out_far.1, s32[8,32]{1,0:T(8,128)} %bitcast.1, ...), custom_call_target="tpu_custom_call" | custom-call | tf_op jit(solution)/shard_map/step/pallas_call | solution.py:901
  96.2 1.6 %split.1 = (bf16[128,256]{1,0:T(8,128)(2,1)}, bf16[128,256]{1,0:T(8,128)(2,1)}, bf16[128,256]{1,0:T(8,128)(2,1)}, bf16[256,128]{1,0:T(8,128)(2,1)}) custom-call(bf16[3,128,256]{2,1,0:T(8,128)(2,1)} %get-tuple-element.6.tall_sums, bf16[256,128]{1,0:T(8,128)(2,1)} %get-tuple-element.7.wide_sums), custom_call_target="tpu_custom_call" | custom-call | tf_op jit(solution)/shard_map/split/pallas_call | solution.py:918
